TPU v7x, 32 devices: a whole 2x2x4 slice. The times are simulated.
32 devices in a mesh: beam: 2 (over y), height: 4 (over x, core), angles: 4 (over z).
Axes of the slice: x: 2, y: 2, z: 4, core: 2. Of those that a mesh axis runs over, the one named last changes fastest.
Arguments:
- element_maps: float32 [24, 4, 32, 256], P(None, 'height', 'beam'), may hold values from 0.1 to 1
- angles: int32 [8], P('angles'), may hold values from 0 to 95
- absorb_incident: float32 [24], replicated, may hold values from 0.0003 to 0.003
- absorb_table: float32 [32, 24], replicated, may hold values from 0.0003 to 0.003
- line_index: int32 [24], replicated, may hold values from 0 to 31
- measured: float32 [8, 24, 4, 256], P('angles', None, 'height'), may hold values from 0 to 1
Outputs:
- updated_maps: float32 [24, 4, 32, 256], P(None, 'height', 'beam')
- residual: float32 [8, 24, 4, 256], P('angles', None, 'height')
All inputs are finite; a program needn't handle non-finite values.
Results may differ from a plain program's by a relative error of at most 0.0003.
Values sent between devices are 32-bit elements; how exact they have to be, the bound alone decides.
A program may use at most 64 MiB of HBM per device.

v0:
```python
import functools
import math

import jax
import jax.numpy as jnp
from jax import lax
from jax.experimental import pallas as pl
from jax.experimental.pallas import tpu as pltpu
from jax.sharding import PartitionSpec as P

WINDOW = 96
ITERS = 2
EPSILON = 1e-06
STEP_SIZE = 0.05
DETECT_SCALE = 1.0 / 32.0
HIGHEST = lax.Precision.HIGHEST
MESH = pl.DeviceIdType.MESH
F32 = jnp.float32
BF16 = jnp.bfloat16
GROUP = 8


def split(value):
    high = value.astype(BF16)
    return high, (value - high.astype(F32)).astype(BF16)


def dot(left, right):
    return jnp.dot(left, right, preferred_element_type=F32)


def mix(high_ref, low_ref, value):
    high, low = split(value)
    return dot(high_ref[...], high) + (dot(low_ref[...], high) + dot(high_ref[...], low))


def spread(value, sums):
    high, low = split(value)
    return dot(high, sums) + dot(low, sums)


def kernel(
    sizes,
    maps_ref, info_ref, measured_ref, incident_ref,
    out_high, out_low, back_high, back_low, exit_ref, enter_ref,
    current, residual_ref,
    shifted, info, seen, scalars, coef0, coef1, sampled, fading, slabs, misfit,
    acc0, acc1, squares,
    local_sem, info_send, info_recv, seen_send, seen_recv,
    slab_send, slab_recv, norm_send, norm_recv,
):
    beams, heights, groups = sizes
    elems, width = maps_ref.shape[1:]
    depth = maps_ref.shape[0]
    mine = info_ref.shape[0]
    total_angles = groups * mine
    xgroups = depth // GROUP
    rows = GROUP * elems
    beam = lax.axis_index("beam")
    height = lax.axis_index("height")
    group = lax.axis_index("angles")
    plane = beams * heights
    place = beam * heights + height
    cells = float(elems * depth * width * plane)

    def plane_id(index):
        return (index // heights, lax.rem(index, heights), group)

    barrier = pltpu.get_barrier_semaphore()
    for step in range(1, groups):
        pl.semaphore_signal(
            barrier, inc=1, device_id=(beam, height, lax.rem(group + step, groups)), device_id_type=MESH
        )

    @pl.loop(1, plane)
    def _(step):
        pl.semaphore_signal(
            barrier, inc=1, device_id=plane_id(lax.rem(place + step, plane)), device_id_type=MESH
        )

    pl.semaphore_wait(barrier, groups - 1 + plane - 1)

    def info_copy(step, slot):
        peer = lax.rem(group + step, groups)
        part = pl.ds(slot * mine, mine)
        return pltpu.make_async_remote_copy(
            info_ref, info.at[part], info_send.at[peer], info_recv.at[slot],
            device_id=(beam, height, peer), device_id_type=MESH,
        )

    def seen_copy(step, slot):
        peer = lax.rem(group + step, groups)
        part = pl.ds(slot * mine, mine)
        return pltpu.make_async_remote_copy(
            measured_ref, seen.at[part], seen_send.at[peer], seen_recv.at[slot],
            device_id=(beam, height, peer), device_id_type=MESH,
        )

    for step in range(1, groups):
        info_copy(step, group).start()
    for step in range(1, groups):
        seen_copy(step, group).start()
    info[pl.ds(group * mine, mine)] = info_ref[...]
    seen[pl.ds(group * mine, mine)] = measured_ref[...]

    for x in range(depth):
        plane_x = maps_ref[x]
        current[x] = plane_x
        shifted[x] = pltpu.roll(plane_x, width - 1, 1)

    for step in range(1, groups):
        copy = info_copy(step, lax.rem(group + step, groups))
        copy.wait_send()
        copy.wait_recv()
    fill = pltpu.make_async_copy(info, scalars, local_sem)
    fill.start()
    fill.wait()

    def slab_copy(iteration, a, step, slot):
        peer = lax.rem(beam + step, beams)
        return pltpu.make_async_remote_copy(
            slabs.at[iteration, beam, a], slabs.at[iteration, slot, a],
            slab_send.at[iteration, peer, a], slab_recv.at[iteration, slot, a],
            device_id=(peer, height, group), device_id_type=MESH,
        )

    def norm_copy(iteration, step, slot):
        peer = lax.rem(place + step, plane)
        return pltpu.make_async_remote_copy(
            squares.at[iteration, place], squares.at[iteration, slot],
            norm_send.at[iteration, peer], norm_recv.at[iteration, slot],
            device_id=plane_id(peer), device_id_type=MESH,
        )

    def forward(iteration, a):
        cols = info[a]
        start = jnp.broadcast_to(cols[:, 0:1], (depth, width))
        fraction = cols[:, 1:2]
        path = cols[0:1, 2:3]
        position = lax.broadcasted_iota(jnp.int32, (depth, width), 1).astype(F32)
        below = start < 0
        inside = (below & (position <= (width - 1) + start)) | (~below & (position >= start))
        edge = below & (position == width - 1) & (start >= -width)
        inner = inside & (position <= width - 2)
        coef0[a] = jnp.where(inside, 1.0 - fraction, 0.0)
        coef1[a] = jnp.where(inner | edge, fraction, 0.0)
        carry = jnp.zeros((1, width), F32)
        total = jnp.zeros((elems, width), F32)
        for g in range(xgroups):
            for xi in range(GROUP):
                x = g * GROUP + xi
                blend = coef0[a, x : x + 1] * current[x] + coef1[a, x : x + 1] * shifted[x]
                shift = scalars[a, x, 3].astype(jnp.int32)
                sampled[a, x * elems : (x + 1) * elems] = pltpu.roll(blend, shift, 1)
            mu = mix(out_high, out_low, sampled[a, g * rows : (g + 1) * rows])
            depth_in = path * mu[rows : rows + GROUP] + carry
            carry = carry + path * mu[rows + GROUP : rows + GROUP + 1]
            tau = spread(mu[:rows], exit_ref[...])
            for xi in range(GROUP):
                x = g * GROUP + xi
                fade = jnp.exp(-(tau[xi * elems : (xi + 1) * elems] + depth_in[xi : xi + 1]))
                fading[a, x * elems : (x + 1) * elems] = fade
                total = total + fade * sampled[a, x * elems : (x + 1) * elems]
        slabs[iteration, beam, a, 0:elems] = (path * DETECT_SCALE) * total
        slabs[iteration, beam, a, elems : elems + 8] = jnp.broadcast_to(carry, (8, width))
        for step in range(1, beams):
            slab_copy(iteration, a, step, beam).start()

    def backward(iteration, a):
        for step in range(1, beams):
            copy = slab_copy(iteration, a, step, lax.rem(beam + step, beams))
            copy.wait_send()
            copy.wait_recv()
        cols = info[a]
        path = cols[0:1, 2:3]
        before = jnp.zeros((1, width), F32)
        scale = jnp.zeros((1, width), F32)
        fluor = jnp.zeros((elems, width), F32)
        after = jnp.zeros((elems, width), F32)
        for b in range(beams):
            dim = jnp.exp(-before)
            part = dim * slabs[iteration, b, a, 0:elems]
            fluor = fluor + part
            after = after + jnp.where(b > beam, 1.0, 0.0) * part
            scale = scale + jnp.where(b == beam, 1.0, 0.0) * dim
            before = before + slabs[iteration, b, a, elems : elems + 1]
        residual = fluor - seen[a]
        misfit[a] = residual
        carry = jnp.sum(residual * after, axis=0, keepdims=True)
        source = residual * (scale * (path * DETECT_SCALE))
        incident = path * incident_ref[...]
        for g in reversed(range(xgroups)):
            emitted = []
            for xi in range(GROUP):
                x = g * GROUP + xi
                part = slice(x * elems, (x + 1) * elems)
                emitted.append(source * fading[a, part] * sampled[a, part])
            mixed = mix(back_high, back_low, jnp.concatenate(emitted, axis=0))
            behind = mixed[rows : rows + GROUP] + carry
            carry = carry + mixed[rows + GROUP : rows + GROUP + 1]
            back = spread(mixed[:rows], enter_ref[...])
            for xi in range(GROUP):
                x = g * GROUP + xi
                weighted = source * fading[a, x * elems : (x + 1) * elems]
                grad = (
                    weighted
                    - incident * behind[xi : xi + 1]
                    - back[xi * elems : (xi + 1) * elems]
                )
                shift = scalars[a, x, 4].astype(jnp.int32)
                grad = pltpu.roll(grad, shift, 1)
                acc0[x] = acc0[x] + coef0[a, x : x + 1] * grad
                acc1[x] = acc1[x] + coef1[a, x : x + 1] * grad

    @pl.loop(0, ITERS)
    def _(iteration):
        @pl.loop(0, total_angles)
        def _(a):
            forward(iteration, a)

        @pl.when(iteration == 0)
        def _():
            for step in range(1, groups):
                copy = seen_copy(step, lax.rem(group + step, groups))
                copy.wait_send()
                copy.wait_recv()

        acc0[...] = jnp.zeros_like(acc0)
        acc1[...] = jnp.zeros_like(acc1)

        @pl.loop(0, total_angles)
        def _(a):
            backward(iteration, a)

        square = jnp.zeros((8, width), F32)
        for x in range(depth):
            grad = acc0[x] + pltpu.roll(acc1[x], 1, 1)
            acc0[x] = grad
            grad = grad * grad
            for row in range(0, elems, 8):
                square = square + grad[row : row + 8]
        folded = square[:, 0:128]
        for lane in range(128, width, 128):
            folded = folded + square[:, lane : lane + 128]
        squares[iteration, place] = folded

        @pl.loop(1, plane)
        def _(step):
            norm_copy(iteration, step, place).start()

        @pl.loop(1, plane)
        def _(step):
            copy = norm_copy(iteration, step, lax.rem(place + step, plane))
            copy.wait_send()
            copy.wait_recv()

        whole = jnp.sum(squares[iteration], axis=0)
        whole = jnp.sum(jnp.sum(whole, axis=0, keepdims=True), axis=1, keepdims=True)
        rate = STEP_SIZE / jnp.sqrt(whole / cells + EPSILON)
        for x in range(depth):
            plane_x = current[x] - rate * acc0[x]
            current[x] = plane_x
            shifted[x] = pltpu.roll(plane_x, width - 1, 1)

    residual_ref[...] = misfit[pl.ds(group * mine, mine)]


def shards(element_maps, angles, absorb_incident, absorb_table, line_index, measured):
    elems, height_rows, depth, width = element_maps.shape
    beams = lax.axis_size("beam")
    heights = lax.axis_size("height")
    groups = lax.axis_size("angles")
    mine = angles.shape[0]
    total_angles = groups * mine
    line_total = depth * beams
    rows = GROUP * elems

    pick_line = (line_index[:, None] == jnp.arange(absorb_table.shape[0])[None, :]).astype(F32)
    absorb_out = jnp.dot(pick_line, absorb_table, precision=HIGHEST)
    eye = jnp.eye(GROUP, dtype=F32)
    places = jnp.arange(GROUP)
    earlier = (places[:, None] > places[None, :]).astype(F32) + 0.5 * eye
    ones = jnp.ones((8, GROUP), F32)

    def stack(table, sums, vector):
        body = (eye[:, None, :, None] * table[None, :, None, :]).reshape(rows, rows)
        tail = jnp.concatenate([sums, ones], axis=0)
        tail = (tail[:, :, None] * vector[None, None, :]).reshape(GROUP + 8, rows)
        return split(jnp.concatenate([body, tail], axis=0))

    out_high, out_low = stack(absorb_out, earlier, absorb_incident)
    back_high, back_low = stack(absorb_out.T, earlier.T, jnp.ones_like(absorb_incident))
    later = jnp.arange(width)
    exit_sum = (later[:, None] > later[None, :]).astype(F32) + 0.5 * (
        later[:, None] == later[None, :]
    ).astype(F32)

    x_pos = (lax.axis_index("beam") * depth + jnp.arange(depth)).astype(F32) - (line_total - 1) / 2
    angle_rad = ((angles.astype(F32) + 0.5) / WINDOW - 0.5) * (math.pi / 2)
    slopes = jnp.tan(angle_rad)
    path_len = 1.0 / jnp.cos(angle_rad)
    shift = x_pos[None, :] * slopes[:, None]
    start = jnp.floor(shift)
    fraction = shift - start
    lanes = jnp.arange(128)[None, None, :]
    info = jnp.zeros((mine, depth, 128), F32)
    columns = (
        start,
        fraction,
        jnp.broadcast_to(path_len[:, None], start.shape),
        jnp.mod(-start, float(width)),
        jnp.mod(start, float(width)),
    )
    for lane, column in enumerate(columns):
        info = jnp.where(lanes == lane, column[:, :, None], info)

    maps = jnp.transpose(element_maps[:, 0], (1, 0, 2))
    vmem = pl.BlockSpec(memory_space=pltpu.VMEM)
    plane = beams * heights
    updated, residual = pl.pallas_call(
        functools.partial(kernel, (beams, heights, groups)),
        out_shape=(
            jax.ShapeDtypeStruct((depth, elems, width), F32),
            jax.ShapeDtypeStruct((mine, elems, width), F32),
        ),
        in_specs=[vmem] * 10,
        out_specs=(vmem, vmem),
        scratch_shapes=[
            pltpu.VMEM((depth, elems, width), F32),
            pltpu.VMEM((total_angles, depth, 128), F32),
            pltpu.VMEM((total_angles, elems, width), F32),
            pltpu.SMEM((total_angles, depth, 128), F32),
            pltpu.VMEM((total_angles, depth, width), F32),
            pltpu.VMEM((total_angles, depth, width), F32),
            pltpu.VMEM((total_angles, depth * elems, width), F32),
            pltpu.VMEM((total_angles, depth * elems, width), F32),
            pltpu.VMEM((ITERS, beams, total_angles, elems + 8, width), F32),
            pltpu.VMEM((total_angles, elems, width), F32),
            pltpu.VMEM((depth, elems, width), F32),
            pltpu.VMEM((depth, elems, width), F32),
            pltpu.VMEM((ITERS, plane, 8, 128), F32),
            pltpu.SemaphoreType.DMA,
            pltpu.SemaphoreType.DMA((groups,)),
            pltpu.SemaphoreType.DMA((groups,)),
            pltpu.SemaphoreType.DMA((groups,)),
            pltpu.SemaphoreType.DMA((groups,)),
            pltpu.SemaphoreType.DMA((ITERS, beams, total_angles)),
            pltpu.SemaphoreType.DMA((ITERS, beams, total_angles)),
            pltpu.SemaphoreType.DMA((ITERS, plane)),
            pltpu.SemaphoreType.DMA((ITERS, plane)),
        ],
        compiler_params=pltpu.CompilerParams(
            collective_id=0, has_side_effects=True, vmem_limit_bytes=40 * 1024 * 1024
        ),
    )(
        maps, info, measured[:, :, 0], jnp.broadcast_to(absorb_incident[:, None], (elems, width)),
        out_high, out_low, back_high, back_low, exit_sum.astype(BF16), exit_sum.T.astype(BF16),
    )
    return (jnp.transpose(updated, (1, 0, 2))[:, None], residual[:, :, None])


def solution(mesh):
    in_specs = (
        P(None, "height", "beam", None),
        P("angles"),
        P(),
        P(),
        P(),
        P("angles", None, "height", None),
    )
    out_specs = (P(None, "height", "beam", None), P("angles", None, "height", None))
    return jax.shard_map(shards, mesh=mesh, in_specs=in_specs, out_specs=out_specs, check_vma=False)
```

profile of v0, /device:TPU:0, one launch (start us, length us, event | category | flops | bytes accessed | tf_op | source)
XLA Modules:
  0.0 59.6 jit_solution(2248504772665310581)
XLA Ops:
  0.6 0.0 copy-start
  0.6 0.7 %cosine_divide_fusion = (f32[2]{0:T(128)S(1)}, f32[2]{0:T(128)S(1)}) fusion(s32[2]{0:T(128)} %param.7), kind=kLoop, calls=%fused_computation.34 | loop fusion | flops 12 | bytes 24 | tf_op jit(solution)/shard_map/div | solution.py:301
  1.4 0.1 and_select_fusion.1
  1.5 0.0 copy-start.4
  1.5 0.1 select_select_fusion.info_ref
  1.6 0.0 copy-done
  1.6 0.6 copy-done.4
  2.2 0.2 fusion.1
  2.3 0.1 copy.9
  2.4 0.2 broadcast_multiply_fusion
  2.6 0.2 mul.115
  2.9 0.2 mul.126
  3.2 0.1 mul.128
  3.3 0.1 reshape.182
  3.4 0.1 mul.118
  3.5 0.0 copy-start.3
  3.5 0.1 mul.119
  3.6 0.6 copy-done.3
  4.1 0.1 mul.121
  4.3 0.0 copy-start.1
  4.3 0.1 add_convert_fusion
  4.4 0.9 %copy-done.1 = f32[24,1,16,256]{3,2,1,0:T(8,128)S(1)} copy-done((f32[24,1,16,256]{3,2,1,0:T(8,128)S(1)}, f32[24,1,16,256]{3,2,1,0:T(8,128)}, u32[]{:S(2)}) %copy-start.1) | copy-done | bytes 393240
  5.3 0.0 copy-start.2
  5.3 0.2 copy.15
  5.5 0.6 copy-done.2
  6.1 0.1 broadcast_in_dim.106.incident_ref
  6.1 51.9 %shard_map.77 = (f32[16,24,256]{2,1,0:T(8,128)S(1)}, f32[2,24,256]{2,1,0:T(8,128)S(1)}) custom-call(f32[16,24,256]{2,1,0:T(8,128)S(1)} %bitcast.18, f32[2,16,128]{2,1,0:T(8,128)S(1)} %select_select_fusion.info_ref, f32[2,24,256]{2,1,0:T(8,128)S(1)} %bitcast.20, f32[24,256]{1,0:T(8,128)S(1)} %broadcast_in_dim.106.incident_ref, ...), custom_call_target="tpu_custom_call" | custom-call | tf_op jit(solution)/shard_map/pallas_call | solution.py:320
  58.0 0.9 %copy.10 = f32[24,1,16,256]{3,2,1,0:T(8,128)} copy(f32[24,1,16,256]{3,0,2,1:T(8,128)S(1)} %bitcast.19) | data formatting | bytes 786432
  58.9 0.7 %copy.11 = f32[2,24,1,256]{3,2,1,0:T(1,128)} copy(f32[2,24,1,256]{3,1,0,2:T(8,128)S(1)} %bitcast.21) | data formatting | bytes 98304
  (16 shorter events, 0.1 us)
Async XLA Ops:
  0.6 1.0 %copy-start = (f32[32,24]{0,1:T(8,128)S(1)}, f32[32,24]{0,1:T(8,128)}, u32[]{:S(2)}) copy-start(f32[32,24]{0,1:T(8,128)} %param.9) | copy-start | bytes 9220
  1.5 0.7 %copy-start.4 = (s32[24]{0:T(128)S(1)}, s32[24]{0:T(128)}, u32[]{:S(2)}) copy-start(s32[24]{0:T(128)} %param.10) | copy-start | bytes 292
  3.5 0.7 %copy-start.3 = (f32[24]{0:T(128)S(1)}, f32[24]{0:T(128)}, u32[]{:S(2)}) copy-start(f32[24]{0:T(128)} %param.8) | copy-start | bytes 292
  4.3 1.0 %copy-start.1 = (f32[24,1,16,256]{3,2,1,0:T(8,128)S(1)}, f32[24,1,16,256]{3,2,1,0:T(8,128)}, u32[]{:S(2)}) copy-start(f32[24,1,16,256]{3,2,1,0:T(8,128)} %param.6) | copy-start | bytes 1179652
  5.3 0.8 %copy-start.2 = (f32[2,24,1,256]{3,2,1,0:T(1,128)S(1)}, f32[2,24,1,256]{3,2,1,0:T(1,128)}, u32[]{:S(2)}) copy-start(f32[2,24,1,256]{3,2,1,0:T(1,128)} %param.11) | copy-start | bytes 147460
where the time goes:
time: 59.8 us; the launch traced here: 59.6 us
  Pallas kernels  51.9 us (87%)
  local copies, waits for them, and re-layouts  5.45 us (9%)
  other arithmetic  1.25 us (2%)
  between operations  0.81 us (1%)
    pallas_call x1, Pallas kernels, shards(): pl.pallas_call(functools.partial(kernel, (beams, heights, groups)), out_s...  51.9 us
    unnamed x15, local copies, waits for them, and re-layouts  4.4 us

commit v1 on v0

--- a/solution.py
+++ b/solution.py
@@ -34,6 +34,40 @@
     return dot(high_ref[...], high) + (dot(low_ref[...], high) + dot(high_ref[...], low))
 
 
+def mix_once(table_ref, value):
+    return dot(table_ref[...], value.astype(BF16))
+
+
+def spread_once(value, sums):
+    return dot(value.astype(BF16), sums)
+
+
+def tile_blocks(table, rows, elems):
+    lane = lax.broadcasted_iota(jnp.int32, (elems, rows), 1)
+    row = lax.broadcasted_iota(jnp.int32, (elems, rows), 0)
+    repeat = jnp.zeros((elems, rows), F32)
+    for block in range(GROUP):
+        repeat = jnp.where(lane == row + block * elems, 1.0, repeat)
+    tiled = dot(table, repeat.astype(BF16))
+    lane = lax.broadcasted_iota(jnp.int32, tiled.shape, 1)
+    bodies = [
+        jnp.where((lane >= block * elems) & (lane < (block + 1) * elems), tiled, 0.0)[:elems]
+        for block in range(GROUP)
+    ]
+    return tiled, bodies
+
+
+def tail_rows(rows, elems, backward):
+    lane = lax.broadcasted_iota(jnp.int32, (GROUP + 8, rows), 1)
+    row = lax.broadcasted_iota(jnp.int32, (GROUP + 8, rows), 0)
+    block = jnp.zeros((GROUP + 8, rows), jnp.int32)
+    for step in range(1, GROUP):
+        block = block + jnp.where(lane >= step * elems, 1, 0)
+    ahead = block > row if backward else block < row
+    weight = jnp.where(ahead, 1.0, jnp.where(block == row, 0.5, 0.0))
+    return jnp.where(row < GROUP, weight, 1.0)
+
+
 def spread(value, sums):
     high, low = split(value)
     return dot(high, sums) + dot(low, sums)
@@ -41,11 +75,10 @@
 
 def kernel(
     sizes,
-    maps_ref, info_ref, measured_ref, incident_ref,
-    out_high, out_low, back_high, back_low, exit_ref, enter_ref,
+    maps_ref, info_ref, measured_ref, incident_ref, table_ref, turned_ref,
     current, residual_ref,
     shifted, info, seen, scalars, coef0, coef1, sampled, fading, slabs, misfit,
-    acc0, acc1, squares,
+    acc0, acc1, squares, out_high, out_low, back_high, exit_ref, enter_ref,
     local_sem, info_send, info_recv, seen_send, seen_recv,
     slab_send, slab_recv, norm_send, norm_recv,
 ):
@@ -103,6 +136,18 @@
     info[pl.ds(group * mine, mine)] = info_ref[...]
     seen[pl.ds(group * mine, mine)] = measured_ref[...]
 
+    tail = tail_rows(rows, elems, False)
+    for part, out_ref in zip(split(table_ref[...]), (out_high, out_low)):
+        tiled, bodies = tile_blocks(part, rows, elems)
+        incident_rows = jnp.concatenate([tiled[elems:]] * ((GROUP + 8) // 8), axis=0)
+        out_ref[...] = jnp.concatenate(bodies + [tail * incident_rows], axis=0).astype(BF16)
+    _, bodies = tile_blocks(turned_ref[...].astype(BF16), rows, elems)
+    back_high[...] = jnp.concatenate(bodies + [tail_rows(rows, elems, True)], axis=0).astype(BF16)
+    source_at = lax.broadcasted_iota(jnp.int32, (width, width), 0)
+    exit_at = lax.broadcasted_iota(jnp.int32, (width, width), 1)
+    half = jnp.where(source_at == exit_at, 0.5, 0.0)
+    exit_ref[...] = jnp.where(source_at > exit_at, 1.0, half).astype(BF16)
+    enter_ref[...] = jnp.where(source_at < exit_at, 1.0, half).astype(BF16)
     for x in range(depth):
         plane_x = maps_ref[x]
         current[x] = plane_x
@@ -195,10 +240,10 @@
                 x = g * GROUP + xi
                 part = slice(x * elems, (x + 1) * elems)
                 emitted.append(source * fading[a, part] * sampled[a, part])
-            mixed = mix(back_high, back_low, jnp.concatenate(emitted, axis=0))
+            mixed = mix_once(back_high, jnp.concatenate(emitted, axis=0))
             behind = mixed[rows : rows + GROUP] + carry
             carry = carry + mixed[rows + GROUP : rows + GROUP + 1]
-            back = spread(mixed[:rows], enter_ref[...])
+            back = spread_once(mixed[:rows], enter_ref[...])
             for xi in range(GROUP):
                 x = g * GROUP + xi
                 weighted = source * fading[a, x * elems : (x + 1) * elems]
@@ -277,24 +322,9 @@
 
     pick_line = (line_index[:, None] == jnp.arange(absorb_table.shape[0])[None, :]).astype(F32)
     absorb_out = jnp.dot(pick_line, absorb_table, precision=HIGHEST)
-    eye = jnp.eye(GROUP, dtype=F32)
-    places = jnp.arange(GROUP)
-    earlier = (places[:, None] > places[None, :]).astype(F32) + 0.5 * eye
-    ones = jnp.ones((8, GROUP), F32)
-
-    def stack(table, sums, vector):
-        body = (eye[:, None, :, None] * table[None, :, None, :]).reshape(rows, rows)
-        tail = jnp.concatenate([sums, ones], axis=0)
-        tail = (tail[:, :, None] * vector[None, None, :]).reshape(GROUP + 8, rows)
-        return split(jnp.concatenate([body, tail], axis=0))
-
-    out_high, out_low = stack(absorb_out, earlier, absorb_incident)
-    back_high, back_low = stack(absorb_out.T, earlier.T, jnp.ones_like(absorb_incident))
-    later = jnp.arange(width)
-    exit_sum = (later[:, None] > later[None, :]).astype(F32) + 0.5 * (
-        later[:, None] == later[None, :]
-    ).astype(F32)
-
+    table = jnp.concatenate(
+        [absorb_out, jnp.broadcast_to(absorb_incident[None, :], (8, elems))], axis=0
+    )
     x_pos = (lax.axis_index("beam") * depth + jnp.arange(depth)).astype(F32) - (line_total - 1) / 2
     angle_rad = ((angles.astype(F32) + 0.5) / WINDOW - 0.5) * (math.pi / 2)
     slopes = jnp.tan(angle_rad)
@@ -323,7 +353,7 @@
             jax.ShapeDtypeStruct((depth, elems, width), F32),
             jax.ShapeDtypeStruct((mine, elems, width), F32),
         ),
-        in_specs=[vmem] * 10,
+        in_specs=[vmem] * 6,
         out_specs=(vmem, vmem),
         scratch_shapes=[
             pltpu.VMEM((depth, elems, width), F32),
@@ -339,6 +369,11 @@
             pltpu.VMEM((depth, elems, width), F32),
             pltpu.VMEM((depth, elems, width), F32),
             pltpu.VMEM((ITERS, plane, 8, 128), F32),
+            pltpu.VMEM((rows + GROUP + 8, rows), BF16),
+            pltpu.VMEM((rows + GROUP + 8, rows), BF16),
+            pltpu.VMEM((rows + GROUP + 8, rows), BF16),
+            pltpu.VMEM((width, width), BF16),
+            pltpu.VMEM((width, width), BF16),
             pltpu.SemaphoreType.DMA,
             pltpu.SemaphoreType.DMA((groups,)),
             pltpu.SemaphoreType.DMA((groups,)),
@@ -354,7 +389,7 @@
         ),
     )(
         maps, info, measured[:, :, 0], jnp.broadcast_to(absorb_incident[:, None], (elems, width)),
-        out_high, out_low, back_high, back_low, exit_sum.astype(BF16), exit_sum.T.astype(BF16),
+        table, absorb_out.T,
     )
     return (jnp.transpose(updated, (1, 0, 2))[:, None], residual[:, :, None])
 

time: 59.8 us -> 51.5 us (0.86)
  Pallas kernels: 51.9 us -> 44.6 us
  other arithmetic: 1.25 us -> 0.24 us
    pallas_call x1, Pallas kernels: 51.9 us -> 44.6 us  [shards(): pl.pallas_call(functools.partial(kernel, (beams, heights, groups)), out_s...]
    unnamed x15 -> x14, local copies, waits for them, and re-layouts: 4.4 us -> 5.27 us
    mul x7 -> x0, local copies, waits for them, and re-layouts: 0.81 us -> none  [the longest x2 0.49 us: stack(): body = (eye[:, None, :, None] * table[None, :, None, :]).reshape(rows, rows)]
    div x1, other arithmetic: 0.71 us -> 0.05 us  [shards(): path_len = 1.0 / jnp.cos(angle_rad)]
where the time goes in v1:
time: 51.5 us; the launch traced here: 51.2 us
  Pallas kernels  44.6 us (87%)
  local copies, waits for them, and re-layouts  5.42 us (11%)
  between operations  0.73 us (1%)
    pallas_call x1, Pallas kernels, shards(): pl.pallas_call(functools.partial(kernel, (beams, heights, groups)), out_s...  44.6 us
    unnamed x14, local copies, waits for them, and re-layouts  5.27 us

profile of v1, /device:TPU:0, one launch (start us, length us, event | category | flops | bytes accessed | tf_op | source)
XLA Modules:
  0.0 51.2 jit_solution(10315368948500176663)
XLA Ops:
  0.6 0.0 copy-start
  0.7 0.0 copy-start.3
  0.7 0.6 %copy-done.3 = s32[2]{0:T(128)S(1)} copy-done((s32[2]{0:T(128)S(1)}, s32[2]{0:T(128)}, u32[]{:S(2)}) %copy-start.3) | copy-done | bytes 32
  1.4 0.1 and_select_fusion.1
  1.5 0.0 copy-start.2
  1.5 0.6 %copy-done.2 = f32[24]{0:T(128)S(1)} copy-done((f32[24]{0:T(128)S(1)}, f32[24]{0:T(128)}, u32[]{:S(2)}) %copy-start.2) | copy-done | bytes 120
  2.1 0.0 copy-start.4
  2.1 0.1 select_select_fusion.info_ref
  2.2 0.0 copy-done
  2.2 0.6 %copy-done.4 = s32[24]{0:T(128)S(1)} copy-done((s32[24]{0:T(128)S(1)}, s32[24]{0:T(128)}, u32[]{:S(2)}) %copy-start.4) | copy-done | bytes 120
  2.8 0.2 fusion
  3.0 0.0 copy-start.1
  3.0 0.1 copy.9
  3.1 0.1 broadcast_in_dim.98.incident_ref
  3.2 0.6 %copy-done.1 = f32[2,24,1,256]{3,2,1,0:T(1,128)S(1)} copy-done((f32[2,24,1,256]{3,2,1,0:T(1,128)S(1)}, f32[2,24,1,256]{3,2,1,0:T(1,128)}, u32[]{:S(2)}) %copy-start.1) | copy-done | bytes 49176
  3.8 1.2 %copy.15 = f32[24,1,16,256]{3,0,2,1:T(8,128)S(1)} copy(f32[24,1,16,256]{3,2,1,0:T(8,128)} %param.6) | data formatting | bytes 786432 | tf_op args[0]
  5.0 44.6 %shard_map.77 = (f32[16,24,256]{2,1,0:T(8,128)S(1)}, f32[2,24,256]{2,1,0:T(8,128)S(1)}) custom-call(f32[16,24,256]{2,1,0:T(8,128)S(1)} %bitcast.14, f32[2,16,128]{2,1,0:T(8,128)S(1)} %select_select_fusion.info_ref, f32[2,24,256]{2,1,0:T(8,128)S(1)} %bitcast.16, f32[24,256]{1,0:T(8,128)S(1)} %broadcast_in_dim.98.incident_ref, ...), custom_call_target="tpu_custom_call" | custom-call | tf_op jit(solution)/shard_map/pallas_call | solution.py:350
  49.7 0.9 %copy.10 = f32[24,1,16,256]{3,2,1,0:T(8,128)} copy(f32[24,1,16,256]{3,0,2,1:T(8,128)S(1)} %bitcast.15) | data formatting | bytes 786432
  50.5 0.7 %copy.11 = f32[2,24,1,256]{3,2,1,0:T(1,128)} copy(f32[2,24,1,256]{3,1,0,2:T(8,128)S(1)} %bitcast.17) | data formatting | bytes 98304
  (8 shorter events, 0.1 us)
Async XLA Ops:
  0.6 1.6 %copy-start = (f32[32,24]{0,1:T(8,128)S(1)}, f32[32,24]{0,1:T(8,128)}, u32[]{:S(2)}) copy-start(f32[32,24]{0,1:T(8,128)} %param.9) | copy-start | bytes 9220
  0.7 0.7 %copy-start.3 = (s32[2]{0:T(128)S(1)}, s32[2]{0:T(128)}, u32[]{:S(2)}) copy-start(s32[2]{0:T(128)} %param.7) | copy-start | bytes 28
  1.5 0.7 %copy-start.2 = (f32[24]{0:T(128)S(1)}, f32[24]{0:T(128)}, u32[]{:S(2)}) copy-start(f32[24]{0:T(128)} %param.8) | copy-start | bytes 292
  2.1 0.7 %copy-start.4 = (s32[24]{0:T(128)S(1)}, s32[24]{0:T(128)}, u32[]{:S(2)}) copy-start(s32[24]{0:T(128)} %param.10) | copy-start | bytes 292
  3.0 0.8 %copy-start.1 = (f32[2,24,1,256]{3,2,1,0:T(1,128)S(1)}, f32[2,24,1,256]{3,2,1,0:T(1,128)}, u32[]{:S(2)}) copy-start(f32[2,24,1,256]{3,2,1,0:T(1,128)} %param.11) | copy-start | bytes 147460

commit v2 on v1

--- a/solution.py
+++ b/solution.py
@@ -79,15 +79,15 @@
     current, residual_ref,
     shifted, info, seen, scalars, coef0, coef1, sampled, fading, slabs, misfit,
     acc0, acc1, squares, out_high, out_low, back_high, exit_ref, enter_ref,
-    local_sem, info_send, info_recv, seen_send, seen_recv,
+    local_sem, maps_sem, info_send, info_recv, seen_send, seen_recv,
     slab_send, slab_recv, norm_send, norm_recv,
 ):
     beams, heights, groups = sizes
-    elems, width = maps_ref.shape[1:]
-    depth = maps_ref.shape[0]
+    elems, depth, width = maps_ref.shape
     mine = info_ref.shape[0]
     total_angles = groups * mine
     xgroups = depth // GROUP
+    pairs = math.gcd(total_angles, 2)
     rows = GROUP * elems
     beam = lax.axis_index("beam")
     height = lax.axis_index("height")
@@ -136,6 +136,11 @@
     info[pl.ds(group * mine, mine)] = info_ref[...]
     seen[pl.ds(group * mine, mine)] = measured_ref[...]
 
+    fetches = [
+        pltpu.make_async_copy(maps_ref.at[:, x], current.at[x], maps_sem.at[x]) for x in range(depth)
+    ]
+    for fetch in fetches:
+        fetch.start()
     tail = tail_rows(rows, elems, False)
     for part, out_ref in zip(split(table_ref[...]), (out_high, out_low)):
         tiled, bodies = tile_blocks(part, rows, elems)
@@ -149,9 +154,8 @@
     exit_ref[...] = jnp.where(source_at > exit_at, 1.0, half).astype(BF16)
     enter_ref[...] = jnp.where(source_at < exit_at, 1.0, half).astype(BF16)
     for x in range(depth):
-        plane_x = maps_ref[x]
-        current[x] = plane_x
-        shifted[x] = pltpu.roll(plane_x, width - 1, 1)
+        fetches[x].wait()
+        shifted[x] = pltpu.roll(current[x], width - 1, 1)
 
     for step in range(1, groups):
         copy = info_copy(step, lax.rem(group + step, groups))
@@ -189,27 +193,35 @@
         inner = inside & (position <= width - 2)
         coef0[a] = jnp.where(inside, 1.0 - fraction, 0.0)
         coef1[a] = jnp.where(inner | edge, fraction, 0.0)
-        carry = jnp.zeros((1, width), F32)
-        total = jnp.zeros((elems, width), F32)
+        for x in range(depth):
+            blend = coef0[a, x : x + 1] * current[x] + coef1[a, x : x + 1] * shifted[x]
+            shift = scalars[a, x, 3].astype(jnp.int32)
+            sampled[a, x * elems : (x + 1) * elems] = pltpu.roll(blend, shift, 1)
+        return path
+
+    def forward_pair(iteration, pair):
+        paths = [forward(iteration, a) for a in pair]
+        carries = [jnp.zeros((1, width), F32) for _ in pair]
+        totals = [jnp.zeros((elems, width), F32) for _ in pair]
         for g in range(xgroups):
-            for xi in range(GROUP):
-                x = g * GROUP + xi
-                blend = coef0[a, x : x + 1] * current[x] + coef1[a, x : x + 1] * shifted[x]
-                shift = scalars[a, x, 3].astype(jnp.int32)
-                sampled[a, x * elems : (x + 1) * elems] = pltpu.roll(blend, shift, 1)
-            mu = mix(out_high, out_low, sampled[a, g * rows : (g + 1) * rows])
-            depth_in = path * mu[rows : rows + GROUP] + carry
-            carry = carry + path * mu[rows + GROUP : rows + GROUP + 1]
-            tau = spread(mu[:rows], exit_ref[...])
-            for xi in range(GROUP):
-                x = g * GROUP + xi
-                fade = jnp.exp(-(tau[xi * elems : (xi + 1) * elems] + depth_in[xi : xi + 1]))
-                fading[a, x * elems : (x + 1) * elems] = fade
-                total = total + fade * sampled[a, x * elems : (x + 1) * elems]
-        slabs[iteration, beam, a, 0:elems] = (path * DETECT_SCALE) * total
-        slabs[iteration, beam, a, elems : elems + 8] = jnp.broadcast_to(carry, (8, width))
-        for step in range(1, beams):
-            slab_copy(iteration, a, step, beam).start()
+            depths = []
+            for n, a in enumerate(pair):
+                mu = mix(out_high, out_low, sampled[a, g * rows : (g + 1) * rows])
+                depth_in = paths[n] * mu[rows : rows + GROUP] + carries[n]
+                carries[n] = carries[n] + paths[n] * mu[rows + GROUP : rows + GROUP + 1]
+                depths.append((depth_in, spread(mu[:rows], exit_ref[...])))
+            for n, a in enumerate(pair):
+                depth_in, tau = depths[n]
+                for xi in range(GROUP):
+                    part = slice((g * GROUP + xi) * elems, (g * GROUP + xi + 1) * elems)
+                    fade = jnp.exp(-(tau[xi * elems : (xi + 1) * elems] + depth_in[xi : xi + 1]))
+                    fading[a, part] = fade
+                    totals[n] = totals[n] + fade * sampled[a, part]
+        for n, a in enumerate(pair):
+            slabs[iteration, beam, a, 0:elems] = (paths[n] * DETECT_SCALE) * totals[n]
+            slabs[iteration, beam, a, elems : elems + 8] = jnp.broadcast_to(carries[n], (8, width))
+            for step in range(1, beams):
+                slab_copy(iteration, a, step, beam).start()
 
     def backward(iteration, a):
         for step in range(1, beams):
@@ -234,34 +246,46 @@
         carry = jnp.sum(residual * after, axis=0, keepdims=True)
         source = residual * (scale * (path * DETECT_SCALE))
         incident = path * incident_ref[...]
+        return source, incident, carry
+
+    def backward_pair(iteration, pair):
+        heads = [backward(iteration, a) for a in pair]
+        carries = [head[2] for head in heads]
         for g in reversed(range(xgroups)):
-            emitted = []
+            sensed = []
+            for n, a in enumerate(pair):
+                source = heads[n][0]
+                emitted = []
+                for xi in range(GROUP):
+                    x = g * GROUP + xi
+                    part = slice(x * elems, (x + 1) * elems)
+                    emitted.append(source * fading[a, part] * sampled[a, part])
+                mixed = mix_once(back_high, jnp.concatenate(emitted, axis=0))
+                behind = mixed[rows : rows + GROUP] + carries[n]
+                carries[n] = carries[n] + mixed[rows + GROUP : rows + GROUP + 1]
+                sensed.append((behind, spread_once(mixed[:rows], enter_ref[...])))
             for xi in range(GROUP):
                 x = g * GROUP + xi
-                part = slice(x * elems, (x + 1) * elems)
-                emitted.append(source * fading[a, part] * sampled[a, part])
-            mixed = mix_once(back_high, jnp.concatenate(emitted, axis=0))
-            behind = mixed[rows : rows + GROUP] + carry
-            carry = carry + mixed[rows + GROUP : rows + GROUP + 1]
-            back = spread_once(mixed[:rows], enter_ref[...])
-            for xi in range(GROUP):
-                x = g * GROUP + xi
-                weighted = source * fading[a, x * elems : (x + 1) * elems]
-                grad = (
-                    weighted
-                    - incident * behind[xi : xi + 1]
-                    - back[xi * elems : (xi + 1) * elems]
-                )
-                shift = scalars[a, x, 4].astype(jnp.int32)
-                grad = pltpu.roll(grad, shift, 1)
-                acc0[x] = acc0[x] + coef0[a, x : x + 1] * grad
-                acc1[x] = acc1[x] + coef1[a, x : x + 1] * grad
+                sum0, sum1 = acc0[x], acc1[x]
+                for n, a in enumerate(pair):
+                    source, incident, _ = heads[n]
+                    behind, back = sensed[n]
+                    grad = (
+                        source * fading[a, x * elems : (x + 1) * elems]
+                        - incident * behind[xi : xi + 1]
+                        - back[xi * elems : (xi + 1) * elems]
+                    )
+                    grad = pltpu.roll(grad, scalars[a, x, 4].astype(jnp.int32), 1)
+                    sum0 = sum0 + coef0[a, x : x + 1] * grad
+                    sum1 = sum1 + coef1[a, x : x + 1] * grad
+                acc0[x] = sum0
+                acc1[x] = sum1
 
     @pl.loop(0, ITERS)
     def _(iteration):
-        @pl.loop(0, total_angles)
-        def _(a):
-            forward(iteration, a)
+        @pl.loop(0, total_angles // pairs)
+        def _(step):
+            forward_pair(iteration, [step * pairs + n for n in range(pairs)])
 
         @pl.when(iteration == 0)
         def _():
@@ -273,9 +297,9 @@
         acc0[...] = jnp.zeros_like(acc0)
         acc1[...] = jnp.zeros_like(acc1)
 
-        @pl.loop(0, total_angles)
-        def _(a):
-            backward(iteration, a)
+        @pl.loop(0, total_angles // pairs)
+        def _(step):
+            backward_pair(iteration, [step * pairs + n for n in range(pairs)])
 
         square = jnp.zeros((8, width), F32)
         for x in range(depth):
@@ -344,7 +368,7 @@
     for lane, column in enumerate(columns):
         info = jnp.where(lanes == lane, column[:, :, None], info)
 
-    maps = jnp.transpose(element_maps[:, 0], (1, 0, 2))
+    maps = element_maps[:, 0]
     vmem = pl.BlockSpec(memory_space=pltpu.VMEM)
     plane = beams * heights
     updated, residual = pl.pallas_call(
@@ -353,7 +377,7 @@
             jax.ShapeDtypeStruct((depth, elems, width), F32),
             jax.ShapeDtypeStruct((mine, elems, width), F32),
         ),
-        in_specs=[vmem] * 6,
+        in_specs=[pl.BlockSpec(memory_space=pl.ANY)] + [vmem] * 5,
         out_specs=(vmem, vmem),
         scratch_shapes=[
             pltpu.VMEM((depth, elems, width), F32),
@@ -375,6 +399,7 @@
             pltpu.VMEM((width, width), BF16),
             pltpu.VMEM((width, width), BF16),
             pltpu.SemaphoreType.DMA,
+            pltpu.SemaphoreType.DMA((depth,)),
             pltpu.SemaphoreType.DMA((groups,)),
             pltpu.SemaphoreType.DMA((groups,)),
             pltpu.SemaphoreType.DMA((groups,)),

time: 51.5 us -> 48.3 us (0.938)
  Pallas kernels: 44.6 us -> 41.7 us
    pallas_call x1, Pallas kernels: 44.6 us -> 41.7 us  [shards(): pl.pallas_call(functools.partial(kernel, (beams, heights, groups)), out_s...]
    unnamed x14 -> x15, local copies, waits for them, and re-layouts: 5.27 us -> 5.04 us
where the time goes in v2:
time: 48.3 us; the launch traced here: 48 us
  Pallas kernels  41.7 us (86%)
  local copies, waits for them, and re-layouts  5.18 us (11%)
  between operations  0.73 us (2%)
    pallas_call x1, Pallas kernels, shards(): pl.pallas_call(functools.partial(kernel, (beams, heights, groups)), out_s...  41.7 us
    unnamed x15, local copies, waits for them, and re-layouts  5.04 us

profile of v2, /device:TPU:0, one launch (start us, length us, event | category | flops | bytes accessed | tf_op | source)
XLA Modules:
  0.0 48.0 jit_solution(17721189065789990646)
XLA Ops:
  0.6 0.0 copy-start
  0.7 0.0 copy-start.4
  0.7 0.6 %copy-done.4 = s32[2]{0:T(128)S(1)} copy-done((s32[2]{0:T(128)S(1)}, s32[2]{0:T(128)}, u32[]{:S(2)}) %copy-start.4) | copy-done | bytes 32
  1.4 0.1 and_select_fusion.1
  1.5 0.0 copy-start.3
  1.5 0.6 %copy-done.3 = f32[24]{0:T(128)S(1)} copy-done((f32[24]{0:T(128)S(1)}, f32[24]{0:T(128)}, u32[]{:S(2)}) %copy-start.3) | copy-done | bytes 120
  2.1 0.0 copy-start.5
  2.1 0.1 select_select_fusion.info_ref
  2.2 0.0 copy-done
  2.2 0.6 %copy-done.5 = s32[24]{0:T(128)S(1)} copy-done((s32[24]{0:T(128)S(1)}, s32[24]{0:T(128)}, u32[]{:S(2)}) %copy-start.5) | copy-done | bytes 120
  2.8 0.2 fusion
  3.0 0.0 copy-start.2
  3.0 0.1 copy.8
  3.1 0.1 broadcast_in_dim.98.incident_ref
  3.2 0.6 %copy-done.2 = f32[2,24,1,256]{3,2,1,0:T(1,128)S(1)} copy-done((f32[2,24,1,256]{3,2,1,0:T(1,128)S(1)}, f32[2,24,1,256]{3,2,1,0:T(1,128)}, u32[]{:S(2)}) %copy-start.2) | copy-done | bytes 49176
  3.8 0.0 copy-start.1
  3.8 1.0 %copy-done.1 = f32[24,1,16,256]{3,2,1,0:T(8,128)S(1)} copy-done((f32[24,1,16,256]{3,2,1,0:T(8,128)S(1)}, f32[24,1,16,256]{3,2,1,0:T(8,128)}, u32[]{:S(2)}) %copy-start.1) | copy-done | bytes 393240
  4.8 41.7 %shard_map.77 = (f32[16,24,256]{2,1,0:T(8,128)S(1)}, f32[2,24,256]{2,1,0:T(8,128)S(1)}) custom-call(f32[24,16,256]{2,1,0:T(8,128)S(1)} %bitcast.11, f32[2,16,128]{2,1,0:T(8,128)S(1)} %select_select_fusion.info_ref, f32[2,24,256]{2,1,0:T(8,128)S(1)} %bitcast.12, f32[24,256]{1,0:T(8,128)S(1)} %broadcast_in_dim.98.incident_ref, ...), custom_call_target="tpu_custom_call" | custom-call | tf_op jit(solution)/shard_map/pallas_call | solution.py:374
  46.5 0.9 %copy.9 = f32[24,1,16,256]{3,2,1,0:T(8,128)} copy(f32[24,1,16,256]{3,0,2,1:T(8,128)S(1)} %bitcast.10) | data formatting | bytes 786432
  47.4 0.7 %copy.10 = f32[2,24,1,256]{3,2,1,0:T(1,128)} copy(f32[2,24,1,256]{3,1,0,2:T(8,128)S(1)} %bitcast.13) | data formatting | bytes 98304
  (8 shorter events, 0.1 us)
Async XLA Ops:
  0.6 1.6 %copy-start = (f32[32,24]{0,1:T(8,128)S(1)}, f32[32,24]{0,1:T(8,128)}, u32[]{:S(2)}) copy-start(f32[32,24]{0,1:T(8,128)} %param.9) | copy-start | bytes 9220
  0.7 0.7 %copy-start.4 = (s32[2]{0:T(128)S(1)}, s32[2]{0:T(128)}, u32[]{:S(2)}) copy-start(s32[2]{0:T(128)} %param.7) | copy-start | bytes 28
  1.5 0.7 %copy-start.3 = (f32[24]{0:T(128)S(1)}, f32[24]{0:T(128)}, u32[]{:S(2)}) copy-start(f32[24]{0:T(128)} %param.8) | copy-start | bytes 292
  2.1 0.7 %copy-start.5 = (s32[24]{0:T(128)S(1)}, s32[24]{0:T(128)}, u32[]{:S(2)}) copy-start(s32[24]{0:T(128)} %param.10) | copy-start | bytes 292
  3.0 0.8 %copy-start.2 = (f32[2,24,1,256]{3,2,1,0:T(1,128)S(1)}, f32[2,24,1,256]{3,2,1,0:T(1,128)}, u32[]{:S(2)}) copy-start(f32[2,24,1,256]{3,2,1,0:T(1,128)} %param.11) | copy-start | bytes 147460
  3.8 1.0 %copy-start.1 = (f32[24,1,16,256]{3,2,1,0:T(8,128)S(1)}, f32[24,1,16,256]{3,2,1,0:T(8,128)}, u32[]{:S(2)}) copy-start(f32[24,1,16,256]{3,2,1,0:T(8,128)} %param.6) | copy-start | bytes 1179652

commit v3 on v2

--- a/solution.py
+++ b/solution.py
@@ -87,7 +87,7 @@
     mine = info_ref.shape[0]
     total_angles = groups * mine
     xgroups = depth // GROUP
-    pairs = math.gcd(total_angles, 2)
+    pairs = math.gcd(total_angles, 4)
     rows = GROUP * elems
     beam = lax.axis_index("beam")
     height = lax.axis_index("height")

time: 48.3 us -> 50.3 us (1.041)
  Pallas kernels: 41.7 us -> 43.7 us
    pallas_call x1, Pallas kernels: 41.7 us -> 43.7 us  [shards(): pl.pallas_call(functools.partial(kernel, (beams, heights, groups)), out_s...]
where the time goes in v3:
time: 50.3 us; the launch traced here: 50 us
  Pallas kernels  43.7 us (87%)
  local copies, waits for them, and re-layouts  5.18 us (10%)
  between operations  0.73 us (1%)
    pallas_call x1, Pallas kernels, shards(): pl.pallas_call(functools.partial(kernel, (beams, heights, groups)), out_s...  43.7 us
    unnamed x15, local copies, waits for them, and re-layouts  5.04 us

profile of v3, /device:TPU:0, one launch (start us, length us, event | category | flops | bytes accessed | tf_op | source)
XLA Modules:
  0.0 50.0 jit_solution(17425917977264455940)
XLA Ops:
  0.6 0.0 copy-start
  0.7 0.0 copy-start.4
  0.7 0.6 %copy-done.4 = s32[2]{0:T(128)S(1)} copy-done((s32[2]{0:T(128)S(1)}, s32[2]{0:T(128)}, u32[]{:S(2)}) %copy-start.4) | copy-done | bytes 32
  1.4 0.1 and_select_fusion.1
  1.5 0.0 copy-start.3
  1.5 0.6 %copy-done.3 = f32[24]{0:T(128)S(1)} copy-done((f32[24]{0:T(128)S(1)}, f32[24]{0:T(128)}, u32[]{:S(2)}) %copy-start.3) | copy-done | bytes 120
  2.1 0.0 copy-start.5
  2.1 0.1 select_select_fusion.info_ref
  2.2 0.0 copy-done
  2.2 0.6 %copy-done.5 = s32[24]{0:T(128)S(1)} copy-done((s32[24]{0:T(128)S(1)}, s32[24]{0:T(128)}, u32[]{:S(2)}) %copy-start.5) | copy-done | bytes 120
  2.8 0.2 fusion
  3.0 0.0 copy-start.2
  3.0 0.1 copy.8
  3.1 0.1 broadcast_in_dim.98.incident_ref
  3.2 0.6 %copy-done.2 = f32[2,24,1,256]{3,2,1,0:T(1,128)S(1)} copy-done((f32[2,24,1,256]{3,2,1,0:T(1,128)S(1)}, f32[2,24,1,256]{3,2,1,0:T(1,128)}, u32[]{:S(2)}) %copy-start.2) | copy-done | bytes 49176
  3.8 0.0 copy-start.1
  3.8 1.0 %copy-done.1 = f32[24,1,16,256]{3,2,1,0:T(8,128)S(1)} copy-done((f32[24,1,16,256]{3,2,1,0:T(8,128)S(1)}, f32[24,1,16,256]{3,2,1,0:T(8,128)}, u32[]{:S(2)}) %copy-start.1) | copy-done | bytes 393240
  4.8 43.7 %shard_map.77 = (f32[16,24,256]{2,1,0:T(8,128)S(1)}, f32[2,24,256]{2,1,0:T(8,128)S(1)}) custom-call(f32[24,16,256]{2,1,0:T(8,128)S(1)} %bitcast.11, f32[2,16,128]{2,1,0:T(8,128)S(1)} %select_select_fusion.info_ref, f32[2,24,256]{2,1,0:T(8,128)S(1)} %bitcast.12, f32[24,256]{1,0:T(8,128)S(1)} %broadcast_in_dim.98.incident_ref, ...), custom_call_target="tpu_custom_call" | custom-call | tf_op jit(solution)/shard_map/pallas_call | solution.py:374
  48.5 0.9 %copy.9 = f32[24,1,16,256]{3,2,1,0:T(8,128)} copy(f32[24,1,16,256]{3,0,2,1:T(8,128)S(1)} %bitcast.10) | data formatting | bytes 786432
  49.4 0.7 %copy.10 = f32[2,24,1,256]{3,2,1,0:T(1,128)} copy(f32[2,24,1,256]{3,1,0,2:T(8,128)S(1)} %bitcast.13) | data formatting | bytes 98304
  (8 shorter events, 0.1 us)
Async XLA Ops:
  0.6 1.6 %copy-start = (f32[32,24]{0,1:T(8,128)S(1)}, f32[32,24]{0,1:T(8,128)}, u32[]{:S(2)}) copy-start(f32[32,24]{0,1:T(8,128)} %param.9) | copy-start | bytes 9220
  0.7 0.7 %copy-start.4 = (s32[2]{0:T(128)S(1)}, s32[2]{0:T(128)}, u32[]{:S(2)}) copy-start(s32[2]{0:T(128)} %param.7) | copy-start | bytes 28
  1.5 0.7 %copy-start.3 = (f32[24]{0:T(128)S(1)}, f32[24]{0:T(128)}, u32[]{:S(2)}) copy-start(f32[24]{0:T(128)} %param.8) | copy-start | bytes 292
  2.1 0.7 %copy-start.5 = (s32[24]{0:T(128)S(1)}, s32[24]{0:T(128)}, u32[]{:S(2)}) copy-start(s32[24]{0:T(128)} %param.10) | copy-start | bytes 292
  3.0 0.8 %copy-start.2 = (f32[2,24,1,256]{3,2,1,0:T(1,128)S(1)}, f32[2,24,1,256]{3,2,1,0:T(1,128)}, u32[]{:S(2)}) copy-start(f32[2,24,1,256]{3,2,1,0:T(1,128)} %param.11) | copy-start | bytes 147460
  3.8 1.0 %copy-start.1 = (f32[24,1,16,256]{3,2,1,0:T(8,128)S(1)}, f32[24,1,16,256]{3,2,1,0:T(8,128)}, u32[]{:S(2)}) copy-start(f32[24,1,16,256]{3,2,1,0:T(8,128)} %param.6) | copy-start | bytes 1179652

commit v4 on v3

--- a/solution.py
+++ b/solution.py
@@ -87,7 +87,8 @@
     mine = info_ref.shape[0]
     total_angles = groups * mine
     xgroups = depth // GROUP
-    pairs = math.gcd(total_angles, 4)
+    pairs = math.gcd(mine, 2)
+    turns = mine // pairs
     rows = GROUP * elems
     beam = lax.axis_index("beam")
     height = lax.axis_index("height")
@@ -156,14 +157,6 @@
     for x in range(depth):
         fetches[x].wait()
         shifted[x] = pltpu.roll(current[x], width - 1, 1)
-
-    for step in range(1, groups):
-        copy = info_copy(step, lax.rem(group + step, groups))
-        copy.wait_send()
-        copy.wait_recv()
-    fill = pltpu.make_async_copy(info, scalars, local_sem)
-    fill.start()
-    fill.wait()
 
     def slab_copy(iteration, a, step, slot):
         peer = lax.rem(beam + step, beams)
@@ -285,7 +278,24 @@
     def _(iteration):
         @pl.loop(0, total_angles // pairs)
         def _(step):
-            forward_pair(iteration, [step * pairs + n for n in range(pairs)])
+            first = lax.rem(group * mine + step * pairs, total_angles)
+
+            @pl.when((iteration == 0) & (lax.rem(step, turns) == 0))
+            def _():
+                slot = first // mine
+
+                @pl.when(step >= turns)
+                def _():
+                    copy = info_copy(step // turns, slot)
+                    copy.wait_send()
+                    copy.wait_recv()
+
+                part = pl.ds(slot * mine, mine)
+                fill = pltpu.make_async_copy(info.at[part], scalars.at[part], local_sem)
+                fill.start()
+                fill.wait()
+
+            forward_pair(iteration, [first + n for n in range(pairs)])
 
         @pl.when(iteration == 0)
         def _():

time: 50.3 us -> 50.8 us (level)
  the two profiles are of different devices: /device:TPU:0 before, /device:TPU:11 now
where the time goes in v4:
time: 50.8 us; the launch traced here: 50.6 us
  Pallas kernels  44.2 us (87%)
  local copies, waits for them, and re-layouts  5.18 us (10%)
  between operations  0.73 us (1%)
    pallas_call x1, Pallas kernels, shards(): pl.pallas_call(functools.partial(kernel, (beams, heights, groups)), out_s...  44.2 us
    unnamed x15, local copies, waits for them, and re-layouts  5.04 us

profile of v4, /device:TPU:11, one launch (start us, length us, event | category | flops | bytes accessed | tf_op | source)
XLA Modules:
  0.0 50.6 jit_solution(11289860585708700955)
XLA Ops:
  0.6 0.0 copy-start
  0.7 0.0 copy-start.4
  0.7 0.6 %copy-done.4 = s32[2]{0:T(128)S(1)} copy-done((s32[2]{0:T(128)S(1)}, s32[2]{0:T(128)}, u32[]{:S(2)}) %copy-start.4) | copy-done | bytes 32
  1.4 0.1 and_select_fusion.1
  1.5 0.0 copy-start.3
  1.5 0.6 %copy-done.3 = f32[24]{0:T(128)S(1)} copy-done((f32[24]{0:T(128)S(1)}, f32[24]{0:T(128)}, u32[]{:S(2)}) %copy-start.3) | copy-done | bytes 120
  2.1 0.0 copy-start.5
  2.1 0.1 select_select_fusion.info_ref
  2.2 0.0 copy-done
  2.2 0.6 %copy-done.5 = s32[24]{0:T(128)S(1)} copy-done((s32[24]{0:T(128)S(1)}, s32[24]{0:T(128)}, u32[]{:S(2)}) %copy-start.5) | copy-done | bytes 120
  2.8 0.2 fusion
  3.0 0.0 copy-start.2
  3.0 0.1 copy.8
  3.1 0.1 broadcast_in_dim.98.incident_ref
  3.2 0.6 %copy-done.2 = f32[2,24,1,256]{3,2,1,0:T(1,128)S(1)} copy-done((f32[2,24,1,256]{3,2,1,0:T(1,128)S(1)}, f32[2,24,1,256]{3,2,1,0:T(1,128)}, u32[]{:S(2)}) %copy-start.2) | copy-done | bytes 49176
  3.8 0.0 copy-start.1
  3.8 1.0 %copy-done.1 = f32[24,1,16,256]{3,2,1,0:T(8,128)S(1)} copy-done((f32[24,1,16,256]{3,2,1,0:T(8,128)S(1)}, f32[24,1,16,256]{3,2,1,0:T(8,128)}, u32[]{:S(2)}) %copy-start.1) | copy-done | bytes 393240
  4.8 44.2 %shard_map.77 = (f32[16,24,256]{2,1,0:T(8,128)S(1)}, f32[2,24,256]{2,1,0:T(8,128)S(1)}) custom-call(f32[24,16,256]{2,1,0:T(8,128)S(1)} %bitcast.11, f32[2,16,128]{2,1,0:T(8,128)S(1)} %select_select_fusion.info_ref, f32[2,24,256]{2,1,0:T(8,128)S(1)} %bitcast.12, f32[24,256]{1,0:T(8,128)S(1)} %broadcast_in_dim.98.incident_ref, ...), custom_call_target="tpu_custom_call" | custom-call | tf_op jit(solution)/shard_map/pallas_call | solution.py:384
  49.0 0.9 %copy.9 = f32[24,1,16,256]{3,2,1,0:T(8,128)} copy(f32[24,1,16,256]{3,0,2,1:T(8,128)S(1)} %bitcast.10) | data formatting | bytes 786432
  49.9 0.7 %copy.10 = f32[2,24,1,256]{3,2,1,0:T(1,128)} copy(f32[2,24,1,256]{3,1,0,2:T(8,128)S(1)} %bitcast.13) | data formatting | bytes 98304
  (8 shorter events, 0.1 us)
Async XLA Ops:
  0.6 1.6 %copy-start = (f32[32,24]{0,1:T(8,128)S(1)}, f32[32,24]{0,1:T(8,128)}, u32[]{:S(2)}) copy-start(f32[32,24]{0,1:T(8,128)} %param.9) | copy-start | bytes 9220
  0.7 0.7 %copy-start.4 = (s32[2]{0:T(128)S(1)}, s32[2]{0:T(128)}, u32[]{:S(2)}) copy-start(s32[2]{0:T(128)} %param.7) | copy-start | bytes 28
  1.5 0.7 %copy-start.3 = (f32[24]{0:T(128)S(1)}, f32[24]{0:T(128)}, u32[]{:S(2)}) copy-start(f32[24]{0:T(128)} %param.8) | copy-start | bytes 292
  2.1 0.7 %copy-start.5 = (s32[24]{0:T(128)S(1)}, s32[24]{0:T(128)}, u32[]{:S(2)}) copy-start(s32[24]{0:T(128)} %param.10) | copy-start | bytes 292
  3.0 0.8 %copy-start.2 = (f32[2,24,1,256]{3,2,1,0:T(1,128)S(1)}, f32[2,24,1,256]{3,2,1,0:T(1,128)}, u32[]{:S(2)}) copy-start(f32[2,24,1,256]{3,2,1,0:T(1,128)} %param.11) | copy-start | bytes 147460
  3.8 1.0 %copy-start.1 = (f32[24,1,16,256]{3,2,1,0:T(8,128)S(1)}, f32[24,1,16,256]{3,2,1,0:T(8,128)}, u32[]{:S(2)}) copy-start(f32[24,1,16,256]{3,2,1,0:T(8,128)} %param.6) | copy-start | bytes 1179652

commit v5 on v2

--- a/solution.py
+++ b/solution.py
@@ -111,30 +111,6 @@
             barrier, inc=1, device_id=plane_id(lax.rem(place + step, plane)), device_id_type=MESH
         )
 
-    pl.semaphore_wait(barrier, groups - 1 + plane - 1)
-
-    def info_copy(step, slot):
-        peer = lax.rem(group + step, groups)
-        part = pl.ds(slot * mine, mine)
-        return pltpu.make_async_remote_copy(
-            info_ref, info.at[part], info_send.at[peer], info_recv.at[slot],
-            device_id=(beam, height, peer), device_id_type=MESH,
-        )
-
-    def seen_copy(step, slot):
-        peer = lax.rem(group + step, groups)
-        part = pl.ds(slot * mine, mine)
-        return pltpu.make_async_remote_copy(
-            measured_ref, seen.at[part], seen_send.at[peer], seen_recv.at[slot],
-            device_id=(beam, height, peer), device_id_type=MESH,
-        )
-
-    for step in range(1, groups):
-        info_copy(step, group).start()
-    for step in range(1, groups):
-        seen_copy(step, group).start()
-    info[pl.ds(group * mine, mine)] = info_ref[...]
-    seen[pl.ds(group * mine, mine)] = measured_ref[...]
 
     fetches = [
         pltpu.make_async_copy(maps_ref.at[:, x], current.at[x], maps_sem.at[x]) for x in range(depth)
@@ -146,6 +122,31 @@
         tiled, bodies = tile_blocks(part, rows, elems)
         incident_rows = jnp.concatenate([tiled[elems:]] * ((GROUP + 8) // 8), axis=0)
         out_ref[...] = jnp.concatenate(bodies + [tail * incident_rows], axis=0).astype(BF16)
+    pl.semaphore_wait(barrier, groups - 1 + plane - 1)
+
+    def info_copy(step, slot):
+        peer = lax.rem(group + step, groups)
+        part = pl.ds(slot * mine, mine)
+        return pltpu.make_async_remote_copy(
+            info_ref, info.at[part], info_send.at[peer], info_recv.at[slot],
+            device_id=(beam, height, peer), device_id_type=MESH,
+        )
+
+    def seen_copy(step, slot):
+        peer = lax.rem(group + step, groups)
+        part = pl.ds(slot * mine, mine)
+        return pltpu.make_async_remote_copy(
+            measured_ref, seen.at[part], seen_send.at[peer], seen_recv.at[slot],
+            device_id=(beam, height, peer), device_id_type=MESH,
+        )
+
+    for step in range(1, groups):
+        info_copy(step, group).start()
+    for step in range(1, groups):
+        seen_copy(step, group).start()
+    info[pl.ds(group * mine, mine)] = info_ref[...]
+    seen[pl.ds(group * mine, mine)] = measured_ref[...]
+
     _, bodies = tile_blocks(turned_ref[...].astype(BF16), rows, elems)
     back_high[...] = jnp.concatenate(bodies + [tail_rows(rows, elems, True)], axis=0).astype(BF16)
     source_at = lax.broadcasted_iota(jnp.int32, (width, width), 0)
@@ -410,7 +411,7 @@
             pltpu.SemaphoreType.DMA((ITERS, plane)),
         ],
         compiler_params=pltpu.CompilerParams(
-            collective_id=0, has_side_effects=True, vmem_limit_bytes=40 * 1024 * 1024
+            collective_id=0, has_side_effects=True, vmem_limit_bytes=60 * 1024 * 1024
         ),
     )(
         maps, info, measured[:, :, 0], jnp.broadcast_to(absorb_incident[:, None], (elems, width)),

time: 48.3 us -> 51.3 us (1.062)
  other arithmetic: 0.24 us -> 1.44 us
  Pallas kernels: 41.7 us -> 42.9 us
  local copies, waits for them, and re-layouts: 5.18 us -> 5.75 us
    pallas_call x1, Pallas kernels: 41.7 us -> 42.9 us  [shards(): pl.pallas_call(functools.partial(kernel, (beams, heights, groups)), out_s...]
    broadcast_in_dim x1, local copies, waits for them, and re-layouts: 0.07 us -> 0.68 us  [shards(): jnp.broadcast_to(absorb_incident[:, None], (elems, width))]
    select_n x1, other arithmetic: 0.08 us -> 0.68 us  [shards(): info = jnp.where(lanes == lane, column[:, :, None], info)]
    concatenate x1, other arithmetic: 0.01 us -> 0.6 us  [shards(): jnp.concatenate([absorb_out, jnp.broadcast_to(absorb_incident[None, :], (...]
    unnamed x15 -> x17, local copies, waits for them, and re-layouts: 5.04 us -> 5 us
where the time goes in v5:
time: 51.3 us; the launch traced here: 51 us
  Pallas kernels  42.9 us (84%)
  local copies, waits for them, and re-layouts  5.75 us (11%)
  other arithmetic  1.44 us (3%)
  between operations  0.73 us (1%)
    pallas_call x1, Pallas kernels, shards(): pl.pallas_call(functools.partial(kernel, (beams, heights, groups)), out_s...  42.9 us
    unnamed x17, local copies, waits for them, and re-layouts  5 us

profile of v5, /device:TPU:0, one launch (start us, length us, event | category | flops | bytes accessed | tf_op | source)
XLA Modules:
  0.0 51.0 jit_solution(1476165448375550584)
XLA Ops:
  0.6 0.0 copy-start
  0.7 0.0 copy-start.5
  0.7 0.6 %copy-done.5 = s32[2]{0:T(128)S(1)} copy-done((s32[2]{0:T(128)S(1)}, s32[2]{0:T(128)}, u32[]{:S(2)}) %copy-start.5) | copy-done | bytes 32
  1.4 0.1 and_select_fusion.1
  1.5 0.0 copy-start.4
  1.5 0.6 %copy-done.4 = f32[24]{0:T(128)S(1)} copy-done((f32[24]{0:T(128)S(1)}, f32[24]{0:T(128)}, u32[]{:S(2)}) %copy-start.4) | copy-done | bytes 120
  2.1 0.0 copy-start.6
  2.1 0.7 %select_select_fusion.info_ref = f32[2,16,128]{2,1,0:T(8,128)} fusion(f32[2,16]{1,0:T(2,128)S(1)} %get-tuple-element.11, f32[2,16]{1,0:T(2,128)S(1)} %get-tuple-element.10, f32[2]{0:T(128)S(1)} %get-tuple-element.12, f32[2,16]{1,0:T(2,128)S(1)} %get-tuple-element.9, f32[2,16]{1,0:T(2,128)S(1)} %get-tuple-element.8, pred[128]{0:T(512)(128)(4,1)S(1)} %get-tuple-element.14, ...), kind=kLoop, calls=%fused_computation.2 | loop fusion | flops 20480 | bytes 17544 | tf_op jit(solution)/shard_map/jit(_where)/select_n | solution.py:370
  2.8 0.0 copy-done
  2.8 0.0 copy-done.6
  2.8 0.2 fusion
  3.0 0.0 copy-start.3
  3.0 0.0 copy-start.1
  3.1 0.1 copy.8
  3.1 0.5 copy-done.3
  3.6 0.6 %pad_maximum_fusion.table_ref = f32[32,24]{1,0:T(8,128)} fusion(f32[8,24]{1,0:T(8,128)S(1)} %broadcast_in_dim.99, f32[24,24]{1,0:T(8,128)S(1)} %copy.8), kind=kLoop, calls=%fused_computation.1 | loop fusion | flops 768 | bytes 6144 | tf_op jit(solution)/shard_map/concatenate | solution.py:350
  4.2 0.7 %broadcast_in_dim.98.incident_ref = f32[24,256]{1,0:T(8,128)} broadcast(f32[24]{0:T(128)S(1)} %copy-done.4), dimensions={0} | broadcast | bytes 24672 | tf_op jit(solution)/shard_map/broadcast_in_dim | solution.py:417
  4.9 0.0 copy-done.1
  4.9 0.6 %copy.13 = f32[2,24,1,256]{3,1,2,0:T(8,128)} copy(f32[2,24,1,256]{3,2,1,0:T(1,128)S(1)} %copy-done.1) | data formatting | bytes 98304
  5.5 42.9 %shard_map.77 = (f32[16,24,256]{2,1,0:T(8,128)}, f32[2,24,256]{2,1,0:T(8,128)}) custom-call(f32[24,16,256]{2,1,0:T(8,128)} %bitcast.11, f32[2,16,128]{2,1,0:T(8,128)} %select_select_fusion.info_ref, f32[2,24,256]{2,1,0:T(8,128)} %bitcast.12, f32[24,256]{1,0:T(8,128)} %broadcast_in_dim.98.incident_ref, f32[32,24]{1,0:T(8,128)} %pad_maximum_fusion.table_ref, ...), custom_call_target="tpu_custom_call" | custom-call | tf_op jit(solution)/shard_map/pallas_call | solution.py:375
  48.4 0.0 copy-start.2
  48.4 1.9 %copy.9 = f32[24,1,16,256]{3,2,1,0:T(8,128)} copy(f32[24,1,16,256]{3,0,2,1:T(8,128)} %bitcast.10) | data formatting | bytes 786432
  50.3 0.0 copy-done.2
  50.3 0.7 %copy.10 = f32[2,24,1,256]{3,2,1,0:T(1,128)} copy(f32[2,24,1,256]{3,1,0,2:T(8,128)S(1)} %bitcast.13) | data formatting | bytes 98304
  (6 shorter events, 0.1 us)
Async XLA Ops:
  0.6 2.2 %copy-start = (f32[32,24]{0,1:T(8,128)S(1)}, f32[32,24]{0,1:T(8,128)}, u32[]{:S(2)}) copy-start(f32[32,24]{0,1:T(8,128)} %param.9) | copy-start | bytes 9220
  0.7 0.7 %copy-start.5 = (s32[2]{0:T(128)S(1)}, s32[2]{0:T(128)}, u32[]{:S(2)}) copy-start(s32[2]{0:T(128)} %param.7) | copy-start | bytes 28
  1.5 0.7 %copy-start.4 = (f32[24]{0:T(128)S(1)}, f32[24]{0:T(128)}, u32[]{:S(2)}) copy-start(f32[24]{0:T(128)} %param.8) | copy-start | bytes 292
  2.1 0.7 %copy-start.6 = (s32[24]{0:T(128)S(1)}, s32[24]{0:T(128)}, u32[]{:S(2)}) copy-start(s32[24]{0:T(128)} %param.10) | copy-start | bytes 292
  3.0 0.6 %copy-start.3 = (f32[24,24]{0,1:T(8,128)}, f32[24,24]{0,1:T(8,128)S(1)}, u32[]{:S(2)}) copy-start(f32[24,24]{0,1:T(8,128)S(1)} %fusion) | copy-start | bytes 6916
  3.0 1.9 %copy-start.1 = (f32[2,24,1,256]{3,2,1,0:T(1,128)S(1)}, f32[2,24,1,256]{3,2,1,0:T(1,128)}, u32[]{:S(2)}) copy-start(f32[2,24,1,256]{3,2,1,0:T(1,128)} %param.11) | copy-start | bytes 147460
  48.4 1.9 %copy-start.2 = (f32[2,24,256]{2,1,0:T(8,128)S(1)}, f32[2,24,256]{2,1,0:T(8,128)}, u32[]{:S(2)}) copy-start(f32[2,24,256]{2,1,0:T(8,128)} %get-tuple-element.5) | copy-start | bytes 147460
